TPU v7x, 128 devices: a whole 4x4x4 slice. The times are simulated.
128 devices in a mesh: tm: 32 (over z_lo, y, x), head: 4 (over z_hi, core).
Axes of the slice: x: 4, y: 4, z: 4 (z_hi: 2, z_lo: 2; z = z_hi * 2 + z_lo), core: 2. Of those that a mesh axis runs over, the one named last changes fastest.
Arguments:
- query: bfloat16 [16384, 2560], P('tm', 'head'), may hold values from -5 to 5
- key: bfloat16 [16384, 2560], P('tm', 'head'), may hold values from -5 to 5
- value: bfloat16 [16384, 2560], P('tm', 'head'), may hold values from -6 to 6
- out_weight: bfloat16 [2560, 5120], P('head'), may hold values from -0.125 to 0.125
- grad_out: bfloat16 [16384, 5120], P('tm', 'head'), may hold values from -6 to 6
- sink_frame: int32 [20], P('head'), may hold values from 0 to 1
- window: int32 [20], P('head'), may hold values from 1 to 3
Outputs:
- grad_query: bfloat16 [16384, 2560], P('tm', 'head')
- grad_key: bfloat16 [16384, 2560], P('tm', 'head')
- grad_value: bfloat16 [16384, 2560], P('tm', 'head')
- grad_weight: float32 [2560, 5120], P('head', 'tm')
All inputs are finite; a program needn't handle non-finite values.
Results may differ from a plain program's by a relative error of at most 0.0077.
Values may be sent and summed in bfloat16 or wider, within the bound.
A program may use at most 192 MiB of HBM per device.

v0:
```python
import math

import jax
import jax.numpy as jnp
from jax import lax
from jax.sharding import PartitionSpec as P

TPF = 256
FR_DEV = 2


def from_behind(value, axis, steps):
    count = lax.axis_size(axis)
    first, last = (max(0, -steps), min(count, count - steps))
    return lax.ppermute(value, axis, [(source, source + steps) for source in range(first, last)])


def from_root(block, axis, source):
    block = jnp.where(lax.axis_index(axis) == source, block, jnp.zeros_like(block))
    return lax.psum(block, axis)


def per_device(query, key, value, out_weight, grad_out, sink_frame, window):
    length, width = query.shape
    heads = sink_frame.shape[0]
    head_size = width // heads
    scale = 1.0 / math.sqrt(head_size)
    place = lax.axis_index("tm")
    offsets = jnp.arange(FR_DEV, dtype=jnp.int32)
    query_frames = place * FR_DEV + offsets
    paired_kv = jnp.stack((key, value))
    earlier = from_behind(paired_kv, "tm", 1)
    key_frames = jnp.concatenate((query_frames - FR_DEV, query_frames))
    reach = query_frames[None, :] - window[:, None]
    window_seen = (key_frames[None, None, :] >= 0) & (
        key_frames[None, None, :] <= query_frames[None, :, None]
    )
    window_seen = window_seen & (key_frames[None, None, :] > reach[:, :, None])
    before_window = sink_frame[:, None] <= reach
    sink_kv = from_root(paired_kv, "tm", 0)
    sink_seen = (offsets[None, None, :] == sink_frame[:, None, None]) & before_window[:, :, None]
    visible = jnp.concatenate((window_seen, sink_seen), axis=2)
    blocks = visible.shape[2]
    all_kv = jnp.concatenate((earlier, paired_kv, sink_kv), axis=1)
    keys_all = all_kv[0].reshape(-1, heads, head_size)
    values_all = all_kv[1].reshape(-1, heads, head_size)
    queries = query.reshape(length, heads, head_size)
    scores = (
        jnp.einsum("qhd,khd->hqk", queries, keys_all, preferred_element_type=jnp.float32) * scale
    )
    scores = scores.reshape(heads, FR_DEV, TPF, blocks, TPF)
    masked = jnp.where(visible[:, :, None, :, None], scores, -1e30)
    peak = jnp.max(masked, axis=(3, 4), keepdims=True)
    weights = jnp.exp(masked - peak)
    probs = weights / jnp.sum(weights, axis=(3, 4), keepdims=True)
    probs = probs.reshape(heads, length, blocks * TPF)
    probs_low = probs.astype(jnp.bfloat16)
    attended = jnp.einsum("hqk,khd->qhd", probs_low, values_all, preferred_element_type=jnp.float32)
    attended = attended.astype(jnp.bfloat16).reshape(length, width)
    cotangent = lax.all_gather(grad_out, "head", axis=1, tiled=True)
    grad_att = lax.dot_general(
        cotangent, out_weight, (((1,), (1,)), ((), ())), preferred_element_type=jnp.float32
    ).astype(jnp.bfloat16)
    weight_term = lax.dot_general(
        attended, cotangent, (((0,), (0,)), ((), ())), preferred_element_type=jnp.float32
    )
    grad_weight = lax.psum_scatter(weight_term, "tm", scatter_dimension=1, tiled=True)
    grad_heads = grad_att.reshape(length, heads, head_size)
    grad_probs = jnp.einsum(
        "qhd,khd->hqk", grad_heads, values_all, preferred_element_type=jnp.float32
    )
    delta = jnp.sum(probs * grad_probs, axis=2, keepdims=True)
    grad_scores = (probs * (grad_probs - delta) * scale).astype(jnp.bfloat16)
    grad_query = jnp.einsum(
        "hqk,khd->qhd", grad_scores, keys_all, preferred_element_type=jnp.float32
    )
    grad_query = grad_query.astype(jnp.bfloat16).reshape(length, width)
    grad_keys = jnp.einsum("hqk,qhd->khd", grad_scores, queries, preferred_element_type=jnp.float32)
    grad_values = jnp.einsum(
        "hqk,qhd->khd", probs_low, grad_heads, preferred_element_type=jnp.float32
    )
    returned = from_behind(jnp.stack((grad_keys[:length], grad_values[:length])), "tm", -1)
    grad_key = (
        (grad_keys[length : 2 * length] + returned[0]).reshape(length, width).astype(jnp.bfloat16)
    )
    grad_value = (
        (grad_values[length : 2 * length] + returned[1]).reshape(length, width).astype(jnp.bfloat16)
    )
    return (grad_query, grad_key, grad_value, grad_weight)


def solution(mesh):
    placed = (
        P("tm", "head"),
        P("tm", "head"),
        P("tm", "head"),
        P("head", None),
        P("tm", "head"),
        P("head"),
        P("head"),
    )
    return jax.shard_map(
        per_device,
        mesh=mesh,
        in_specs=placed,
        out_specs=(P("tm", "head"), P("tm", "head"), P("tm", "head"), P("head", "tm")),
        check_vma=False,
    )
```

profile of v0, /device:TPU:96, one launch (start us, length us, event | category | flops | bytes accessed | tf_op | source)
XLA Modules:
  0.0 598.8 jit_solution(5587819794848925410)
XLA Ops:
  8.0 0.0 copy-start.2
  8.0 0.0 copy-start.3
  8.0 0.0 all-reduce.2.cloned.1.call-start
  8.1 1.3 copy.26
  9.4 1.3 copy.27
  10.7 1.2 pad_maximum_fusion.2
  12.0 0.0 all-reduce.2.cloned.1.call-update
  12.0 0.0 all-gather.2.cloned.1.call-start
  12.1 0.5 all-gather.2.cloned.1.call-update
  12.6 0.0 reduce-scatter.2.cloned.1.call-start
  12.6 3.4 collective-permute-start
  16.1 0.1 broadcast_compare_fusion.1
  16.2 0.1 compare_and_fusion.1
  16.2 0.1 iota_compare_fusion
  16.3 0.1 broadcast_and_fusion
  16.4 0.1 broadcast_subtract_fusion
  16.5 0.1 compare_and_fusion
  16.5 0.1 pad_add_fusion
  16.6 3.7 broadcast_in_dim.13
  20.4 16.5 %broadcast_in_dim.14 = pred[5,512,1536]{2,1,0:T(32,128)(4,1)} reshape(pred[5,2,256,6,256]{4,3,2,1,0:T(8,128)(4,1)} %broadcast_in_dim.13) | data formatting | bytes 7864320 | tf_op jit(solution)/shard_map/jit(_where)/broadcast_in_dim | solution.py:52
  36.9 8.3 %copy.31 = pred[5,512,1536]{1,2,0:T(32,128)(4,1)} copy(pred[5,512,1536]{2,1,0:T(32,128)(4,1)} %broadcast_in_dim.14) | data formatting | bytes 7864320 | tf_op jit(solution)/shard_map/jit(_where)/broadcast_in_dim | solution.py:52
  45.2 1.1 copy.28
  46.2 5.9 collective-permute-done
  52.1 272.0 %all-reduce.2.cloned.1.call-done = bf16[2,512,640]{1,2,0:T(8,128)(2,1)} async-done(((bf16[2,512,640]{1,2,0:T(8,128)(2,1)}), bf16[2,512,640]{1,2,0:T(8,128)(2,1)}) %all-reduce.2.cloned.1.call-update) | async-done | bytes 1310736 | tf_op jit(solution)/shard_map/psum | solution.py:20
  324.1 2.0 pad_maximum_fusion
  326.2 0.0 copy-start.1
  326.2 1.5 fusion.42
  327.7 14.2 %fusion.43 = (f32[5,512]{1,0:T(8,128)S(1)}, f32[5,512,1536]{1,2,0:T(8,128)}) fusion(pred[5,512,1536]{1,2,0:T(32,128)(4,1)} %copy.31, bf16[1536,5,128]{0,2,1:T(8,128)(2,1)} %bitcast.75, bf16[512,5,128]{0,2,1:T(8,128)(2,1)S(1)} %bitcast.80), kind=kOutput, calls=%fused_computation.53 | convolution fusion | flops 1022363136 | bytes 22292480 | tf_op jit(solution)/shard_map/sub | solution.py:54
  341.9 10.9 %fusion.24 = bf16[5,128,512]{2,1,0:T(8,128)(2,1)S(1)} fusion(bf16[1536,5,128]{0,2,1:T(8,128)(2,1)S(1)} %bitcast.65, f32[5,512]{1,0:T(8,128)S(1)} %get-tuple-element.22, pred[5,512,1536]{1,2,0:T(32,128)(4,1)} %copy.31, bf16[1536,5,128]{0,2,1:T(8,128)(2,1)} %bitcast.76, bf16[512,5,128]{0,2,1:T(8,128)(2,1)S(1)} %bitcast.81), kind=kOutput, calls=%fused_computation.21 | convolution fusion | flops 2033258496 | bytes 9185280 | tf_op jit(solution)/shard_map/hqk,khd->qhd/dot_general | solution.py:58
  352.8 0.0 all-gather.2.cloned.1.call-done
  352.8 11.5 %fusion.45 = f32[640,5120]{0,1:T(8,128)} fusion(bf16[512,640]{0,1:T(8,128)(2,1)S(1)} %bitcast.79, bf16[512,5120]{1,0:T(8,128)(2,1)} %all-gather.2.cloned.1.call-done), kind=kOutput, calls=%fused_computation.55 | convolution fusion | flops 3355443200 | bytes 19005440 | tf_op jit(solution)/shard_map/dot_general | solution.py:64
  364.3 0.0 reduce-scatter.2.cloned.1.call-update
  364.3 9.5 %convolution_convert_fusion = bf16[512,640]{1,0:T(8,128)(2,1)} fusion(bf16[512,5120]{1,0:T(8,128)(2,1)} %all-gather.2.cloned.1.call-done, bf16[640,5120]{1,0:T(8,128)(2,1)} %param.10), kind=kOutput, calls=%fused_computation.23 | convolution fusion | flops 3355770880 | bytes 12451840 | tf_op jit(solution)/shard_map/dot_general | solution.py:61
  373.9 1.4 copy.32
  375.3 7.8 %fusion.44 = f32[5,512,1536]{1,2,0:T(8,128)} fusion(bf16[512,5,128]{0,2,1:T(8,128)(2,1)S(1)} %bitcast.71, bf16[1536,5,128]{0,2,1:T(8,128)(2,1)S(1)} %bitcast.66), kind=kOutput, calls=%fused_computation.54 | convolution fusion | flops 1006632960 | bytes 18350080 | tf_op jit(solution)/shard_map/qhd,khd->hqk/dot_general | solution.py:69
  383.1 23.9 %fusion.21 = f32[1536,5,128]{0,2,1:T(8,128)} fusion(bf16[512,5,128]{0,2,1:T(8,128)(2,1)S(1)} %bitcast.82, f32[5,512,1536]{1,2,0:T(8,128)} %fusion.44, f32[5,512,1536]{1,2,0:T(8,128)} %get-tuple-element.23, f32[5,512]{1,0:T(8,128)S(1)} %get-tuple-element.22), kind=kOutput, calls=%fused_computation.19 | convolution fusion | flops 1034162176 | bytes 36055040 | tf_op jit(solution)/shard_map/hqk,qhd->khd/dot_general | solution.py:78
  407.0 1.4 slice_bitcast_fusion.3
  408.4 12.7 %fusion.18 = f32[1536,5,128]{0,2,1:T(8,128)} fusion(bf16[512,5,128]{0,2,1:T(8,128)(2,1)S(1)} %bitcast.72, f32[5,512]{1,0:T(8,128)S(1)} %get-tuple-element.22, pred[5,512,1536]{1,2,0:T(32,128)(4,1)} %copy.31, bf16[1536,5,128]{0,2,1:T(8,128)(2,1)} %bitcast.77, bf16[512,5,128]{0,2,1:T(8,128)(2,1)S(1)} %bitcast.83), kind=kOutput, calls=%fused_computation.18 | convolution fusion | flops 2032930816 | bytes 11151360 | tf_op jit(solution)/shard_map/hqk,qhd->khd/dot_general | solution.py:79
  421.1 1.4 slice_bitcast_fusion.2
  422.5 1.9 pad_maximum_fusion.1
  424.4 7.2 %collective-permute-start.1 = (f32[2,512,5,128]{1,3,2,0:T(8,128)}, f32[2,512,5,128]{1,3,2,0:T(8,128)S(1)}, u32[]{:S(2)}, u32[]{:S(2)}) collective-permute-start(f32[2,512,5,128]{1,3,2,0:T(8,128)} %pad_maximum_fusion.1), channel_id=1, source_target_pairs={{4,0},{8,4},{12,8},{16,12},{20,16},{24,20},{28,24},{32,28},{36,32}... | collective-permute-start | bytes 7864328 | tf_op jit(solution)/shard_map/ppermute | solution.py:15
  431.6 22.3 %fusion.27 = bf16[5,128,512]{2,1,0:T(8,128)(2,1)S(1)} fusion(bf16[1536,5,128]{0,2,1:T(8,128)(2,1)} %bitcast.78, f32[5,512,1536]{1,2,0:T(8,128)} %fusion.44, f32[5,512,1536]{1,2,0:T(8,128)} %get-tuple-element.23, f32[5,512]{1,0:T(8,128)S(1)} %get-tuple-element.22), kind=kOutput, calls=%fused_computation.22 | convolution fusion | flops 1034489856 | bytes 34088960 | tf_op jit(solution)/shard_map/hqk,khd->qhd/dot_general | solution.py:74
  454.0 1.1 copy.41
  455.0 82.6 %collective-permute-done.1 = f32[2,512,5,128]{1,3,2,0:T(8,128)S(1)} collective-permute-done((f32[2,512,5,128]{1,3,2,0:T(8,128)}, f32[2,512,5,128]{1,3,2,0:T(8,128)S(1)}, u32[]{:S(2)}, u32[]{:S(2)}) %collective-permute-start.1) | collective-permute-done | bytes 2621472 | tf_op jit(solution)/shard_map/ppermute | solution.py:15
  537.7 3.0 fusion.31
  540.7 2.2 copy.42
  542.8 1.1 copy.43
  543.9 46.9 %reduce-scatter.2.cloned.1.call-done = f32[640,160]{0,1:T(8,128)} async-done(((f32[640,5120]{0,1:T(8,128)}), f32[640,160]{0,1:T(8,128)}) %reduce-scatter.2.cloned.1.call-update) | async-done | bytes 409616 | tf_op jit(solution)/shard_map/reduce_scatter | solution.py:67
  (6 shorter events, 0.0 us)
Async XLA Ops:
  8.0 8.2 %copy-start.2 = (s32[5]{0:T(128)S(1)}, s32[5]{0:T(128)}, u32[]{:S(2)}) copy-start(s32[5]{0:T(128)} %param.13) | copy-start | bytes 64
  8.0 8.2 %copy-start.3 = (s32[5]{0:T(128)S(1)}, s32[5]{0:T(128)}, u32[]{:S(2)}) copy-start(s32[5]{0:T(128)} %param.12) | copy-start | bytes 64
  8.0 316.1 %all-reduce.2.cloned.1.call-start = ((), (), s32[]{:S(2)}) async-start(), calls=%async_computation.1 | async-start | bytes 2621440 | tf_op jit(solution)/shard_map/psum | solution.py:20
  12.0 340.8 %all-gather.2.cloned.1.call-start = ((), (), s32[]{:S(2)}) async-start(), calls=%async_computation.2 | async-start | bytes 6553600 | tf_op jit(solution)/shard_map/all_gather | solution.py:60
  12.6 578.2 %reduce-scatter.2.cloned.1.call-start = ((), (), s32[]{:S(2)}) async-start(), calls=%async_computation.3 | async-start | bytes 13516800 | tf_op jit(solution)/shard_map/reduce_scatter | solution.py:67
  12.6 39.5 %collective-permute-start = (bf16[2,512,640]{1,2,0:T(8,128)(2,1)S(1)}, bf16[2,512,640]{1,2,0:T(8,128)(2,1)}, u32[]{:S(2)}, u32[]{:S(2)}) collective-permute-start(bf16[2,512,640]{1,2,0:T(8,128)(2,1)S(1)} %get-tuple-element.18), channel_id=1, source_target_pairs={{0,4},{4,8},{8,12},{12,16},{16,20},{20,24},{24,28},{28,32},{32,36}... | collective-permute-start | bytes 3932168 | tf_op jit(solution)/shard_map/ppermute | solution.py:15
  36.9 8.3 %copy-start = (bf16[512,640]{1,0:T(8,128)(2,1)S(1)}, bf16[512,640]{1,0:T(8,128)(2,1)}, u32[]{:S(2)}) copy-start(bf16[512,640]{1,0:T(8,128)(2,1)} %param.7) | copy-start | bytes 1966084
  326.2 1.5 copy-start.1
  424.4 113.2 %collective-permute-start.1 = (f32[2,512,5,128]{1,3,2,0:T(8,128)}, f32[2,512,5,128]{1,3,2,0:T(8,128)S(1)}, u32[]{:S(2)}, u32[]{:S(2)}) collective-permute-start(f32[2,512,5,128]{1,3,2,0:T(8,128)} %pad_maximum_fusion.1), channel_id=1, source_target_pairs={{4,0},{8,4},{12,8},{16,12},{20,16},{24,20},{28,24},{32,28},{36,32}... | collective-permute-start | bytes 7864328 | tf_op jit(solution)/shard_map/ppermute | solution.py:15
Sparse Core Ops, SparseCore 0:
  12.1 311.9 all-reduce.1
  364.5 226.3 reduce-scatter.1
Sparse Core Ops, SparseCore 1:
  14.3 46.9 all-gather.1
where the time goes:
time: 605 us; the launch traced here: 599 us
  waiting for transfers between devices  408 us (67%)
  matrix products  113 us (19%)
  local copies, waits for them, and re-layouts  42.4 us (7%)
  between operations  16.1 us (3%)
  starting transfers between devices  10.7 us (2%)
  other arithmetic  8.69 us (1%)
    psum x1, waiting for transfers between devices, from_root(): return lax.psum(block, axis)  272 us
    ppermute x2, waiting for transfers between devices, from_behind(): lax.ppermute(value, axis, [(source, source + steps) for source in range(f...  88.5 us
    reduce_scatter x1, waiting for transfers between devices, per_device(): lax.psum_scatter(weight_term, 'tm', scatter_dimension=1, tiled=True)  46.9 us
    broadcast_in_dim x3, local copies, waits for them, and re-layouts, per_device(): masked = jnp.where(visible[:, :, None, :, None], scores, -1e+30)  28.5 us
    dot_general x1, matrix products, per_device(): jnp.einsum('hqk,qhd->khd', grad_scores, queries, preferred_element_type=j...  23.9 us
    dot_general x1, matrix products, per_device(): jnp.einsum('hqk,khd->qhd', grad_scores, keys_all, preferred_element_type=...  22.3 us
    sub x1, matrix products, per_device(): weights = jnp.exp(masked - peak)  14.2 us
    dot_general x1, matrix products, per_device(): jnp.einsum('hqk,qhd->khd', probs_low, grad_heads, preferred_element_type=...  12.7 us
  transfers between devices with their start and end apart: 5, of which 4 were waited for; matrix products, arithmetic and copies ran while one was open for 25% of the time, Pallas kernels for 0%

commit v1 on v0

v1 whole, which is shorter than its diff:
```python
import math

import jax
import jax.numpy as jnp
from jax import lax
from jax.experimental import pallas as pl
from jax.experimental.pallas import tpu as pltpu
from jax.sharding import PartitionSpec as P

MESH = pl.DeviceIdType.MESH
BF = jnp.bfloat16
F32 = jnp.float32
NT = 32
H = 5
HD = 128
T = 256
L = 2 * T
SCALE = 1.0 / math.sqrt(HD)
SCALE2 = SCALE * math.log2(math.e)
CW = 1280
GC = 4
YB = 640
XB = 160
LAST = ((1,), (1,))


def mm(a, b):
    return lax.dot_general(a, b, (((1,), (0,)), ((), ())), preferred_element_type=F32)


def mmt(a, b):
    return lax.dot_general(a, b, (LAST, ((), ())), preferred_element_type=F32)


def kernel(
    q_ref, k_ref, v_ref, w_ref, g_ref, sink_ref, win_ref,
    dq_ref, dk_ref, dv_ref, wo_ref,
    Q, KV, SB, RB, COT, COTT, W, GA, DO, PR, ATT, YS, YR, YSUM, XS, XR, XK, ZF, ZS, ZR, WO,
    DPS, DPR, DQ, DKV,
    l_sem, w_sem, kv_s, kv_r, zg_s, zg_r, co_s, co_r, cf_s, cf_r, sc_s, sc_r, ag_s, ag_r,
    y_s, y_r, x_s, x_r, z_s, z_r, d_s, d_r, o_sem,
):
    t = lax.axis_index("tm")
    hd = lax.axis_index("head")
    zl, y, x = t // 16, (t // 4) % 4, t % 4
    zh, core = hd // 2, hd % 2
    mate = hd + 1 - 2 * core
    far = (hd + 2) % 4
    far_mate = (mate + 2) % 4

    def remote(src, dst, ss, rs, dev):
        return pltpu.make_async_remote_copy(
            src_ref=src, dst_ref=dst, send_sem=ss, recv_sem=rs, device_id=dev, device_id_type=MESH
        )

    def load_own(n):
        ref = (k_ref, v_ref)[n // H] if n < 2 * H else q_ref
        h = n % H
        dst = KV.at[n // H, h, pl.ds(L, L)] if n < 2 * H else Q.at[h]
        return pltpu.make_async_copy(ref.at[:, pl.ds(h * HD, HD)], dst, l_sem.at[n])

    def load_w(s):
        return pltpu.make_async_copy(w_ref.at[:, pl.ds(s * CW, CW)], W.at[s], w_sem.at[s])

    load_g = pltpu.make_async_copy(g_ref, COT.at[hd], w_sem.at[4])
    for n in range(3 * H):
        load_own(n).start()
    load_g.start()
    for s in range(4):
        load_w(s).start()

    barrier = pltpu.get_barrier_semaphore()

    def greet(i, _):
        pl.semaphore_signal(barrier, inc=1, device_id=((t + i) % NT, hd), device_id_type=MESH)
        return 0

    lax.fori_loop(1, NT, greet, 0)
    pl.semaphore_signal(barrier, inc=1, device_id=(t, mate), device_id_type=MESH)
    pl.semaphore_signal(barrier, inc=1, device_id=(t, far), device_id_type=MESH)
    pl.semaphore_wait(barrier, NT + 1)

    def kv_copy(n, h):
        ref = (k_ref, v_ref)[n]
        return remote(
            ref.at[:, pl.ds(h * HD, HD)], KV.at[n, h, pl.ds(0, L)],
            kv_s.at[n, h], kv_r.at[n, h], ((t + 1) % NT, hd),
        )

    def zg_copy(r):
        rows = pl.ds(r * (L // GC), L // GC)
        return remote(g_ref.at[rows], COT.at[hd, rows], zg_s.at[r], zg_r.at[r], (t, far))

    def zg_wait(r):
        rows = pl.ds(r * (L // GC), L // GC)
        remote(COT.at[far, rows], COT.at[far, rows], zg_s.at[r], zg_r.at[r], (t, far)).wait_recv()

    def cf_copy(r):
        rows = pl.ds(r * (L // GC), L // GC)
        return remote(COT.at[far, rows], COT.at[far, rows], cf_s.at[r], cf_r.at[r], (t, mate))

    def cf_wait(r):
        rows = pl.ds(r * (L // GC), L // GC)
        remote(
            COT.at[far_mate, rows], COT.at[far_mate, rows], cf_s.at[r], cf_r.at[r], (t, mate)
        ).wait_recv()

    co_copy = remote(g_ref, COT.at[hd], co_s, co_r, (t, mate))
    co_arrival = remote(COT.at[mate], COT.at[mate], co_s, co_r, (t, mate))

    co_copy.start()
    for r in range(GC):
        zg_copy(r).start()
    for h in range(H):
        kv_copy(0, h).start()
        kv_copy(1, h).start()

    def piece(buf, i):
        return buf.at[i // 16, :, pl.ds(pl.multiple_of((i % 16) * 16, 16), 16), :]

    for n in range(3 * H):
        load_own(n).wait()

    @pl.when(t == 0)
    def _():
        for h in range(H):
            second = sink_ref[h].astype(F32)
            for n in range(2):
                a = KV[n, h, pl.ds(L, T)].astype(F32)
                b = KV[n, h, pl.ds(L + T, T)].astype(F32)
                RB[n, h] = (a * (1.0 - second) + b * second).astype(BF)
        SB[0, :, pl.ds(0, 16), :] = RB[0, :, pl.ds(0, 16), :]

        def scatter(i, _):
            remote(piece(RB, i), piece(SB, i), sc_s.at[i], sc_r, (i, hd)).start()
            return 0

        lax.fori_loop(1, NT, scatter, 0)

    @pl.when(t != 0)
    def _():
        remote(piece(SB, t), piece(SB, t), sc_s.at[0], sc_r, (0, hd)).wait_recv()

    def ag_copy(i):
        return remote(piece(SB, t), piece(SB, t), ag_s.at[i], ag_r.at[t], ((t + i) % NT, hd))

    def ag_start(i, _):
        ag_copy(i).start()
        return 0

    lax.fori_loop(1, NT, ag_start, 0)

    def use_block(s, first):
        for half in range(2):
            COTT[2 * s + half] = COT[s, :, pl.ds(half * YB, YB)].T

        def rows(m, _):
            at = pl.ds(pl.multiple_of(m * 128, 128), 128)
            got = mmt(COT[s, at], W[s])
            GA[at] = got if first else GA[at] + got
            return 0

        lax.fori_loop(0, L // 128, rows, 0)

    load_g.wait()
    for s in range(4):
        load_w(s).wait()
    use_block(hd, True)
    co_arrival.wait_recv()
    use_block(mate, False)

    def ag_wait(i, _):
        src = (t + i) % NT
        remote(piece(SB, src), piece(SB, src), ag_s.at[i], ag_r.at[src], (src, hd)).wait_recv()
        return 0

    lax.fori_loop(1, NT, ag_wait, 0)

    def biases(h, i):
        f = 2 * t + i
        win, snk = win_ref[h], sink_ref[h]
        off = jnp.float32(-1e30)
        on = jnp.float32(0.0)
        return (
            jnp.where((win >= 3) & (f >= 2), on, off),
            jnp.where((win >= 2) & (f >= 1), on, off),
            None,
            jnp.where(snk <= f - win, on, off),
        )

    def forward(h):
        vt = KV[1, h].T
        svt = SB[1, h].T
        for i in range(2):
            q = Q[h, pl.ds(i * T, T)]
            peak = None
            scores = []
            for b, bias in enumerate(biases(h, i)):
                keys = KV[0, h, pl.ds((i + b) * T, T)] if b < 3 else SB[0, h]
                s = mmt(keys, q) * SCALE2
                if bias is not None:
                    s = s + bias
                top = jnp.max(s, axis=0, keepdims=True)
                peak = top if peak is None else jnp.maximum(peak, top)
                scores.append(s)
            weights = [jnp.exp2(s - peak) for s in scores]
            total = sum(jnp.sum(e, axis=0, keepdims=True) for e in weights)
            inverse = 1.0 / total
            out = None
            for b, e in enumerate(weights):
                p = e * inverse
                PR[2 * h + i, pl.ds(b * T, T)] = p
                values = vt[:, (i + b) * T : (i + b + 1) * T] if b < 3 else svt
                term = mm(values, p.astype(BF))
                out = term if out is None else out + term
            ATT[h, :, pl.ds(i * T, T)] = out.astype(BF)

    def d_copy(h):
        return remote(DPS.at[h], DPR.at[h], d_s.at[h], d_r.at[h], ((t + NT - 1) % NT, hd))

    def out_copy(n, h):
        ref = (dq_ref, dk_ref, dv_ref)[n]
        src = DQ.at[h] if n == 0 else DKV.at[n - 1, h]
        return pltpu.make_async_copy(src, ref.at[:, pl.ds(pl.multiple_of(h * HD, HD), HD)], o_sem.at[n, h])

    def backward(h):
        kt = KV[0, h].T
        skt = SB[0, h].T
        near = []
        for i in range(2):
            q = Q[h, pl.ds(i * T, T)]
            do = DO[h, pl.ds(i * T, T)]
            grads = []
            delta = None
            for b in range(4):
                values = KV[1, h, pl.ds((i + b) * T, T)] if b < 3 else SB[1, h]
                dp = mmt(values, do)
                term = jnp.sum(PR[2 * h + i, pl.ds(b * T, T)] * dp, axis=0, keepdims=True)
                delta = term if delta is None else delta + term
                grads.append(dp)
            out = None
            terms = []
            for b in range(4):
                p = PR[2 * h + i, pl.ds(b * T, T)]
                ds = (p * (grads[b] - delta) * SCALE).astype(BF)
                keys = kt[:, (i + b) * T : (i + b + 1) * T] if b < 3 else skt
                term = mm(keys, ds)
                out = term if out is None else out + term
                if b < 3:
                    terms.append((mm(ds, q), mm(p.astype(BF), do)))
            DQ[h, pl.ds(i * T, T)] = out.T.astype(BF)
            near.append(terms)
        out_copy(0, h).start()
        for n in range(2):
            DPS[h, n, pl.ds(0, T)] = near[0][0][n].astype(BF)
            DPS[h, n, pl.ds(T, T)] = (near[0][1][n] + near[1][0][n]).astype(BF)
            PR[2 * h, pl.ds(0, T), pl.ds(n * HD, HD)] = near[0][2][n] + near[1][1][n]
            PR[2 * h, pl.ds(T, T), pl.ds(n * HD, HD)] = near[1][2][n]
        d_copy(h).start()

    def finish_kv(h):
        d_copy(h).wait_recv()
        for n in range(2):
            own = PR[2 * h, pl.ds(0, L), pl.ds(n * HD, HD)]
            DKV[n, h] = (own + DPR[h, n].astype(F32)).astype(BF)
            out_copy(n + 1, h).start()

    def which(j):
        g = (zh + j // H) % 2
        h = j % H
        return g, h, 1 - 2 * ((g + h) % 2)

    def part(g, yy, h):
        return mmt(COTT[g * 4 + yy], ATT[h])

    def y_copy(j, m):
        _, _, d = which(j)
        to = (y + (d if m != 1 else -d) + 4) % 4
        return remote(YS.at[j, m], YR.at[j, m], y_s.at[j, m], y_r.at[j, m], (zl * 16 + to * 4 + x, hd))

    def x_copy(j, m):
        _, _, d = which(j)
        to = (x + (d if m != 1 else -d) + 4) % 4
        return remote(XS.at[j, m], XR.at[j, m], x_s.at[j, m], x_r.at[j, m], (zl * 16 + y * 4 + to, hd))

    def z_copy(h):
        return remote(ZS.at[h], ZR.at[h], z_s.at[h], z_r.at[h], ((t + 16) % NT, hd))

    def step1(j):
        g, h, d = which(j)
        YS[j, 0] = part(g, (y + 2) % 4, h).astype(BF)
        y_copy(j, 0).start()
        YS[j, 1] = part(g, (y - d + 4) % 4, h).astype(BF)
        y_copy(j, 1).start()

    def step2(j):
        g, h, d = which(j)
        own = part(g, (y + d + 4) % 4, h)
        y_copy(j, 0).wait_recv()
        YS[j, 2] = (own + YR[j, 0].astype(F32)).astype(BF)
        y_copy(j, 2).start()

    def x_rows(xx):
        return pl.ds(pl.multiple_of(xx * XB, XB), XB)

    def step3(j):
        g, h, d = which(j)
        own = part(g, y, h)
        y_copy(j, 1).wait_recv()
        y_copy(j, 2).wait_recv()
        YSUM[...] = own + YR[j, 1].astype(F32) + YR[j, 2].astype(F32)
        XS[j, 0] = YSUM[x_rows((x + 2) % 4)].astype(BF)
        x_copy(j, 0).start()
        XS[j, 1] = YSUM[x_rows((x - d + 4) % 4)].astype(BF)
        x_copy(j, 1).start()
        XK[j, 0] = YSUM[x_rows((x + d + 4) % 4)]
        XK[j, 1] = YSUM[x_rows(x)]

    def step4(j):
        x_copy(j, 0).wait_recv()
        XS[j, 2] = (XK[j, 0] + XR[j, 0].astype(F32)).astype(BF)
        x_copy(j, 2).start()

    def step5(j):
        g, h, _ = which(j)
        x_copy(j, 1).wait_recv()
        x_copy(j, 2).wait_recv()
        ZF[g, h] = XK[j, 1] + XR[j, 1].astype(F32) + XR[j, 2].astype(F32)

        @pl.when(j >= H)
        def _():
            ZS[h] = ZF[1 - zl, h].astype(BF)
            z_copy(h).start()

    def step6(h):
        z_copy(h).wait_recv()
        WO[h] = ZF[zl, h] + ZR[h].astype(F32)

    def turn(j, _):
        @pl.when(j < GC)
        def _():
            zg_wait(j)
            cf_copy(j).start()

        @pl.when(j < H)
        def _():
            for n in range(2):
                remote(
                    KV.at[n, j, pl.ds(0, L)], KV.at[n, j, pl.ds(0, L)],
                    kv_s.at[n, j], kv_r.at[n, j], ((t + 1) % NT, hd),
                ).wait_recv()
            forward(j)

        @pl.when(j == H)
        def _():
            use_block(far, False)
            for r in range(GC):
                cf_wait(r)
            use_block(far_mate, False)
            for h in range(H):
                DO[h] = GA[:, h * HD : (h + 1) * HD].astype(BF)

        @pl.when(j < 2 * H)
        def _():
            step1(j)

        @pl.when((j >= 1) & (j < 2 * H + 1))
        def _():
            step2(j - 1)

        @pl.when((j >= H) & (j < 2 * H))
        def _():
            backward(j - H)

        @pl.when((j >= 2) & (j < 2 * H + 2))
        def _():
            step3(j - 2)

        @pl.when((j >= 3) & (j < 2 * H + 3))
        def _():
            step4(j - 3)

        @pl.when((j >= H + 2) & (j < 2 * H + 2))
        def _():
            finish_kv(j - H - 2)

        @pl.when((j >= 4) & (j < 2 * H + 4))
        def _():
            step5(j - 4)

        @pl.when(j >= H + 5)
        def _():
            step6(j - H - 5)

        return 0

    lax.fori_loop(0, 2 * H + 5, turn, 0)
    put_w = pltpu.make_async_copy(WO, wo_ref, w_sem.at[4])
    put_w.start()

    co_copy.wait_send()
    for r in range(GC):
        zg_copy(r).wait_send()
        cf_copy(r).wait_send()

    @pl.when(t == 0)
    def _():
        def sent(i, _):
            remote(piece(RB, i), piece(SB, i), sc_s.at[i], sc_r, (i, hd)).wait_send()
            return 0

        lax.fori_loop(1, NT, sent, 0)

    def ag_sent(i, _):
        ag_copy(i).wait_send()
        return 0

    lax.fori_loop(1, NT, ag_sent, 0)

    def rs_sent(j, _):
        for m in range(3):
            y_copy(j, m).wait_send()
            x_copy(j, m).wait_send()
        return 0

    lax.fori_loop(0, 2 * H, rs_sent, 0)
    for h in range(H):
        kv_copy(0, h).wait_send()
        kv_copy(1, h).wait_send()
        z_copy(h).wait_send()
        d_copy(h).wait_send()
        for n in range(3):
            out_copy(n, h).wait()
    put_w.wait()


def per_device(query, key, value, out_weight, grad_out, sink_frame, window):
    dma = pltpu.SemaphoreType.DMA
    any_spec = pl.BlockSpec(memory_space=pl.ANY)
    smem = pl.BlockSpec(memory_space=pltpu.SMEM)
    sds = jax.ShapeDtypeStruct
    grad_query, grad_key, grad_value, weight = pl.pallas_call(
        kernel,
        out_shape=[sds((L, H * HD), BF)] * 3 + [sds((H, XB, HD), F32)],
        in_specs=[any_spec] * 5 + [smem] * 2,
        out_specs=[any_spec] * 4,
        scratch_shapes=[
            pltpu.VMEM((H, L, HD), BF),
            pltpu.VMEM((2, H, 2 * L, HD), BF),
            pltpu.VMEM((2, H, T, HD), BF),
            pltpu.VMEM((2, H, T, HD), BF),
            pltpu.VMEM((4, L, CW), BF),
            pltpu.VMEM((8, YB, L), BF),
            pltpu.VMEM((4, H * HD, CW), BF),
            pltpu.VMEM((L, H * HD), F32),
            pltpu.VMEM((H, L, HD), BF),
            pltpu.VMEM((2 * H, 4 * T, T), F32),
            pltpu.VMEM((H, HD, L), BF),
            pltpu.VMEM((2 * H, 3, YB, HD), BF),
            pltpu.VMEM((2 * H, 3, YB, HD), BF),
            pltpu.VMEM((YB, HD), F32),
            pltpu.VMEM((2 * H, 3, XB, HD), BF),
            pltpu.VMEM((2 * H, 3, XB, HD), BF),
            pltpu.VMEM((2 * H, 2, XB, HD), F32),
            pltpu.VMEM((2, H, XB, HD), F32),
            pltpu.VMEM((H, XB, HD), BF),
            pltpu.VMEM((H, XB, HD), BF),
            pltpu.VMEM((H, XB, HD), F32),
            pltpu.VMEM((H, 2, L, HD), BF),
            pltpu.VMEM((H, 2, L, HD), BF),
            pltpu.VMEM((H, L, HD), BF),
            pltpu.VMEM((2, H, L, HD), BF),
            dma((3 * H,)), dma((5,)),
            dma((2, H)), dma((2, H)),
            dma((GC,)), dma((GC,)),
            dma, dma,
            dma((GC,)), dma((GC,)),
            dma((NT,)), dma,
            dma((NT,)), dma((NT,)),
            dma((2 * H, 3)), dma((2 * H, 3)),
            dma((2 * H, 3)), dma((2 * H, 3)),
            dma((H,)), dma((H,)),
            dma((H,)), dma((H,)),
            dma((3, H)),
        ],
        compiler_params=pltpu.CompilerParams(
            collective_id=0, has_side_effects=True, vmem_limit_bytes=60 * 1024 * 1024
        ),
        name="layer_backward",
    )(query, key, value, out_weight, grad_out, sink_frame, window)
    grad_weight = jnp.swapaxes(weight, 1, 2).reshape(H * HD, XB)
    return (grad_query, grad_key, grad_value, grad_weight)


def solution(mesh):
    placed = (
        P("tm", "head"),
        P("tm", "head"),
        P("tm", "head"),
        P("head", None),
        P("tm", "head"),
        P("head"),
        P("head"),
    )
    return jax.shard_map(
        per_device,
        mesh=mesh,
        in_specs=placed,
        out_specs=(P("tm", "head"), P("tm", "head"), P("tm", "head"), P("head", "tm")),
        check_vma=False,
    )
```

time: 605 us -> 194 us (0.32)
  waiting for transfers between devices: 408 us -> 0 us
  Pallas kernels: 0 us -> 185 us
  matrix products: 113 us -> 0 us
  local copies, waits for them, and re-layouts: 42.4 us -> 7.72 us
  between operations: 16.1 us -> 0.64 us
  starting transfers between devices: 10.7 us -> 0 us
  other arithmetic: 8.69 us -> 0 us
    psum x1 -> x0, waiting for transfers between devices: 272 us -> none  [from_root(): return lax.psum(block, axis)]
    pallas_call x0 -> x1, Pallas kernels: none -> 185 us  [per_device(): pl.pallas_call(kernel, out_shape=[sds((L, H * HD), BF)] * 3 + [sds((H, XB...]
    dot_general x7 -> x0, matrix products: 98.6 us -> none  [the longest x1 23.9 us: per_device(): jnp.einsum('hqk,qhd->khd', grad_scores, queries, preferred_element_type=j...]
    ppermute x2 -> x0, waiting for transfers between devices: 88.5 us -> none  [from_behind(): lax.ppermute(value, axis, [(source, source + steps) for source in range(f...]
    reduce_scatter x1 -> x0, waiting for transfers between devices: 46.9 us -> none  [per_device(): lax.psum_scatter(weight_term, 'tm', scatter_dimension=1, tiled=True)]
    broadcast_in_dim x3 -> x0, local copies, waits for them, and re-layouts: 28.5 us -> none  [per_device(): masked = jnp.where(visible[:, :, None, :, None], scores, -1e+30)]
    sub x1 -> x0, matrix products: 14.2 us -> none  [per_device(): weights = jnp.exp(masked - peak)]
    ppermute x2 -> x0, starting transfers between devices: 10.6 us -> none  [from_behind(): lax.ppermute(value, axis, [(source, source + steps) for source in range(f...]
  transfers between devices with their start and end apart: 5 -> 0, of which waited for: 4 -> 0; matrix products, arithmetic and copies ran while one was open for 25% -> 0% of each run, Pallas kernels for 0% -> 0%
where the time goes in v1:
time: 194 us
  Pallas kernels  185 us (95%)
  local copies, waits for them, and re-layouts  7.72 us (4%)
    pallas_call x1, Pallas kernels, per_device(): pl.pallas_call(kernel, out_shape=[sds((L, H * HD), BF)] * 3 + [sds((H, XB...  185 us
    unnamed x3, local copies, waits for them, and re-layouts  5.94 us

profile of v1, /device:TPU:96, one launch (start us, length us, event | category | flops | bytes accessed | tf_op | source)
XLA Modules:
  0.0 193.6 jit_solution(4378162310931383074)
XLA Ops:
  0.6 185.3 %layer_backward.1 = (bf16[512,640]{1,0:T(8,128)(2,1)}, bf16[512,640]{1,0:T(8,128)(2,1)}, bf16[512,640]{1,0:T(8,128)(2,1)}, f32[5,160,128]{2,1,0:T(8,128)}) custom-call(bf16[512,640]{1,0:T(8,128)(2,1)} %q_ref.1, bf16[512,640]{1,0:T(8,128)(2,1)} %k_ref.1, bf16[512,640]{1,0:T(8,128)(2,1)} %v_ref.1, bf16[640,5120]{1,0:T(8,128)(2,1)} %w_ref.1, ...), custom_call_target="tpu_custom_call" | custom-call | tf_op jit(solution)/shard_map/layer_backward/pallas_call | solution.py:442
  185.9 1.8 copy_bitcast_fusion
  187.7 2.0 %copy.17 = bf16[512,640]{1,0:T(8,128)(2,1)} copy(bf16[512,640]{1,0:T(8,128)(2,1)} %get-tuple-element.16) | data formatting | bytes 1310720
  189.7 2.0 %copy.18 = bf16[512,640]{1,0:T(8,128)(2,1)} copy(bf16[512,640]{1,0:T(8,128)(2,1)} %get-tuple-element.17) | data formatting | bytes 1310720
  191.7 2.0 %copy.19 = bf16[512,640]{1,0:T(8,128)(2,1)} copy(bf16[512,640]{1,0:T(8,128)(2,1)} %get-tuple-element.18) | data formatting | bytes 1310720

commit v2 on v1

--- a/solution.py
+++ b/solution.py
@@ -10,6 +10,7 @@
 MESH = pl.DeviceIdType.MESH
 BF = jnp.bfloat16
 F32 = jnp.float32
+NP = 16
 NT = 32
 H = 5
 HD = 128
@@ -22,6 +23,10 @@
 YB = 640
 XB = 160
 LAST = ((1,), (1,))
+EARLY_ZG = 0
+Z_RELAY = {1: 17, 2: 20, 3: 28, 4: 19}
+X_FIRST = (1, 3)
+EARLY_PLUS = 3
 
 
 def mm(a, b):
@@ -35,9 +40,9 @@
 def kernel(
     q_ref, k_ref, v_ref, w_ref, g_ref, sink_ref, win_ref,
     dq_ref, dk_ref, dv_ref, wo_ref,
-    Q, KV, SB, RB, COT, COTT, W, GA, DO, PR, ATT, YS, YR, YSUM, XS, XR, XK, ZF, ZS, ZR, WO,
+    Q, KV, SB, RB, RL, RLD, COT, COTT, W, GA, PR, ATT, YS, YR, YSUM, XS, XR, XK, ZF, ZS, ZR, WO,
     DPS, DPR, DQ, DKV,
-    l_sem, w_sem, kv_s, kv_r, zg_s, zg_r, co_s, co_r, cf_s, cf_r, sc_s, sc_r, ag_s, ag_r,
+    l_sem, w_sem, kv_s, kv_r, rl_r, rl_s, rd_r, rd_s, zg_s, zg_r, co_s, co_r, cf_s, cf_r, sc_s, sc_r, ag_s, ag_r,
     y_s, y_r, x_s, x_r, z_s, z_r, d_s, d_r, o_sem,
 ):
     t = lax.axis_index("tm")
@@ -80,12 +85,39 @@
     pl.semaphore_signal(barrier, inc=1, device_id=(t, far), device_id_type=MESH)
     pl.semaphore_wait(barrier, NT + 1)
 
-    def kv_copy(n, h):
-        ref = (k_ref, v_ref)[n]
-        return remote(
-            ref.at[:, pl.ds(h * HD, HD)], KV.at[n, h, pl.ds(0, L)],
-            kv_s.at[n, h], kv_r.at[n, h], ((t + 1) % NT, hd),
-        )
+    row_end = (x == 3) & (y < 3)
+    plane_end = t == NT // 2 - 1
+    row_relay = (x == 3) & (y > 0)
+
+    def kv_copies(n, h):
+        src = (k_ref, v_ref)[n].at[:, pl.ds(h * HD, HD)]
+        sem = kv_s.at[n, h]
+        out = []
+        direct = t < NT - 1
+        if h >= 3:
+            out.append((row_end, remote(src, RL.at[h - 3, n], sem, rl_r.at[h - 3, n], (t + 4, hd))))
+            direct = direct & jnp.logical_not(row_end)
+        if h in Z_RELAY:
+            to = Z_RELAY[h]
+            out.append((plane_end, remote(src, RL.at[0, n], sem, rl_r.at[0, n], (to, hd))))
+            direct = direct & jnp.logical_not(plane_end)
+        place = KV.at[n, h, pl.ds(0, L)]
+        out.append((direct, remote(src, place, sem, kv_r.at[n, h], ((t + 1) % NT, hd))))
+        return out
+
+    def kv_relays():
+        roles = [(row_relay, 0, 3, (t + NT - 3) % NT, 1), (row_relay, 1, 4, (t + NT - 3) % NT, 2)]
+        roles += [(t == at, 0, h, NT // 2, h - 1) for h, at in Z_RELAY.items()]
+        for mine, slot, h, to, turn in roles:
+            for n in range(2):
+                yield turn, mine, remote(
+                    RL.at[slot, n], KV.at[n, h, pl.ds(0, L)], rl_s.at[slot, n], kv_r.at[n, h], (to, hd)
+                ), remote(RL.at[slot, n], RL.at[slot, n], rl_s.at[slot, n], rl_r.at[slot, n], (to, hd))
+
+    def when(condition, act):
+        @pl.when(condition)
+        def _():
+            act()
 
     def zg_copy(r):
         rows = pl.ds(r * (L // GC), L // GC)
@@ -108,15 +140,19 @@
     co_copy = remote(g_ref, COT.at[hd], co_s, co_r, (t, mate))
     co_arrival = remote(COT.at[mate], COT.at[mate], co_s, co_r, (t, mate))
 
+    def send_kv(h, first):
+        for n in range(2):
+            copies = kv_copies(n, h)
+            for condition, copy in copies[:-1] if first else copies[-1:]:
+                when(condition, copy.start)
+
     co_copy.start()
-    for r in range(GC):
+    for r in range(EARLY_ZG):
         zg_copy(r).start()
-    for h in range(H):
-        kv_copy(0, h).start()
-        kv_copy(1, h).start()
 
     def piece(buf, i):
-        return buf.at[i // 16, :, pl.ds(pl.multiple_of((i % 16) * 16, 16), 16), :]
+        i = i % NP
+        return buf.at[i // 8, :, pl.ds(pl.multiple_of((i % 8) * 32, 32), 32), :]
 
     for n in range(3 * H):
         load_own(n).wait()
@@ -129,38 +165,52 @@
                 a = KV[n, h, pl.ds(L, T)].astype(F32)
                 b = KV[n, h, pl.ds(L + T, T)].astype(F32)
                 RB[n, h] = (a * (1.0 - second) + b * second).astype(BF)
-        SB[0, :, pl.ds(0, 16), :] = RB[0, :, pl.ds(0, 16), :]
+        SB[0, :, pl.ds(0, 32), :] = RB[0, :, pl.ds(0, 32), :]
 
         def scatter(i, _):
             remote(piece(RB, i), piece(SB, i), sc_s.at[i], sc_r, (i, hd)).start()
             return 0
 
-        lax.fori_loop(1, NT, scatter, 0)
+        lax.fori_loop(1, NP, scatter, 0)
 
     @pl.when(t != 0)
     def _():
-        remote(piece(SB, t), piece(SB, t), sc_s.at[0], sc_r, (0, hd)).wait_recv()
+        remote(piece(SB, t), piece(SB, t), sc_s.at[1], sc_r, (0, hd)).wait_recv()
+
+    over = remote(piece(SB, t), piece(SB, t), sc_s.at[0], sc_r, ((t + NP) % NT, hd))
+    when(zl == 0, over.start)
 
     def ag_copy(i):
-        return remote(piece(SB, t), piece(SB, t), ag_s.at[i], ag_r.at[t], ((t + i) % NT, hd))
+        to = zl * NP + (t + i) % NP
+        return remote(piece(SB, t), piece(SB, t), ag_s.at[i], ag_r.at[t % NP], (to, hd))
 
     def ag_start(i, _):
         ag_copy(i).start()
         return 0
 
-    lax.fori_loop(1, NT, ag_start, 0)
+    lax.fori_loop(1, NP, ag_start, 0)
+    for r in range(EARLY_ZG, GC):
+        zg_copy(r).start()
+    for h in (3, 4, 1, 2):
+        send_kv(h, True)
+    for h in range(H):
+        send_kv(h, False)
+
+    def use_rows(s, r, first=False):
+        rows = pl.ds(pl.multiple_of(r * (L // GC), L // GC), L // GC)
+        for half in range(2):
+            turned = COT[s, rows, pl.ds(half * YB, YB)].T
+            for i in range(4):
+                COTT[2 * s + half, i, :, rows] = turned[i * XB : (i + 1) * XB]
+        got = mmt(COT[s, rows], W[s])
+        GA[rows] = got if first else GA[rows] + got
 
     def use_block(s, first):
-        for half in range(2):
-            COTT[2 * s + half] = COT[s, :, pl.ds(half * YB, YB)].T
-
-        def rows(m, _):
-            at = pl.ds(pl.multiple_of(m * 128, 128), 128)
-            got = mmt(COT[s, at], W[s])
-            GA[at] = got if first else GA[at] + got
+        def body(r, _):
+            use_rows(s, r, first)
             return 0
 
-        lax.fori_loop(0, L // 128, rows, 0)
+        lax.fori_loop(0, GC, body, 0)
 
     load_g.wait()
     for s in range(4):
@@ -170,11 +220,15 @@
     use_block(mate, False)
 
     def ag_wait(i, _):
-        src = (t + i) % NT
-        remote(piece(SB, src), piece(SB, src), ag_s.at[i], ag_r.at[src], (src, hd)).wait_recv()
+        src = zl * NP + (t + i) % NP
+        remote(piece(SB, src), piece(SB, src), ag_s.at[i], ag_r.at[src % NP], (src, hd)).wait_recv()
         return 0
 
-    lax.fori_loop(1, NT, ag_wait, 0)
+    lax.fori_loop(1, NP, ag_wait, 0)
+
+    @pl.when(t == 0)
+    def _():
+        KV[:, :, pl.ds(0, L)] = jnp.zeros((2, H, L, HD), BF)
 
     def biases(h, i):
         f = 2 * t + i
@@ -215,8 +269,17 @@
                 out = term if out is None else out + term
             ATT[h, :, pl.ds(i * T, T)] = out.astype(BF)
 
-    def d_copy(h):
+    row_start = (x == 0) & (y > 0)
+    row_relay_back = (x == 0) & (y < 3)
+
+    def d_direct(h):
         return remote(DPS.at[h], DPR.at[h], d_s.at[h], d_r.at[h], ((t + NT - 1) % NT, hd))
+
+    def d_first(h):
+        return remote(DPS.at[h], RLD.at[h - 3], d_s.at[h], rd_r.at[h - 3], ((t + NT - 4) % NT, hd))
+
+    def d_onward(h):
+        return remote(RLD.at[h - 3], DPR.at[h], rd_s.at[h - 3], d_r.at[h], ((t + 3) % NT, hd))
 
     def out_copy(n, h):
         ref = (dq_ref, dk_ref, dv_ref)[n]
@@ -229,7 +292,7 @@
         near = []
         for i in range(2):
             q = Q[h, pl.ds(i * T, T)]
-            do = DO[h, pl.ds(i * T, T)]
+            do = GA[pl.ds(i * T, T), pl.ds(pl.multiple_of(h * HD, HD), HD)].astype(BF)
             grads = []
             delta = None
             for b in range(4):
@@ -256,46 +319,62 @@
             DPS[h, n, pl.ds(T, T)] = (near[0][1][n] + near[1][0][n]).astype(BF)
             PR[2 * h, pl.ds(0, T), pl.ds(n * HD, HD)] = near[0][2][n] + near[1][1][n]
             PR[2 * h, pl.ds(T, T), pl.ds(n * HD, HD)] = near[1][2][n]
-        d_copy(h).start()
+        when((t > 0) & jnp.logical_not(row_start & (h >= 3)), lambda: d_direct(h).start())
+        when(row_start & (h >= 3), lambda: d_first(h).start())
 
     def finish_kv(h):
-        d_copy(h).wait_recv()
+        @pl.when(t < NT - 1)
+        def _():
+            d_direct(h).wait_recv()
+
+        @pl.when(t == NT - 1)
+        def _():
+            DPR[h] = jnp.zeros((2, L, HD), BF)
+
         for n in range(2):
             own = PR[2 * h, pl.ds(0, L), pl.ds(n * HD, HD)]
             DKV[n, h] = (own + DPR[h, n].astype(F32)).astype(BF)
             out_copy(n + 1, h).start()
 
     def which(j):
-        g = (zh + j // H) % 2
         h = j % H
-        return g, h, 1 - 2 * ((g + h) % 2)
-
-    def part(g, yy, h):
-        return mmt(COTT[g * 4 + yy], ATT[h])
+        turned = (j >= H) & ((h == X_FIRST[0]) | (h == X_FIRST[1]))
+        return (zh + j // H) % 2, h, turned, jnp.where(turned, x, y), jnp.where(turned, y, x)
+
+    def way(j):
+        return jnp.where((j < H) & (j != EARLY_PLUS), -1, 1)
+
+    def part(j, at):
+        g, h, turned, _, _ = which(j)
+        rows = jnp.concatenate(
+            [COTT[g * 4 + jnp.where(turned, i, at), jnp.where(turned, at, i)] for i in range(4)]
+        )
+        return mmt(rows, ATT[h])
 
     def y_copy(j, m):
-        _, _, d = which(j)
-        to = (y + (d if m != 1 else -d) + 4) % 4
-        return remote(YS.at[j, m], YR.at[j, m], y_s.at[j, m], y_r.at[j, m], (zl * 16 + to * 4 + x, hd))
+        _, _, turned, y1, _ = which(j)
+        to = (y1 + (way(j) if m != 1 else -way(j)) + 4) % 4
+        dev = zl * 16 + jnp.where(turned, y * 4 + to, to * 4 + x)
+        return remote(YS.at[j, m], YR.at[j, m], y_s.at[j, m], y_r.at[j, m], (dev, hd))
 
     def x_copy(j, m):
-        _, _, d = which(j)
-        to = (x + (d if m != 1 else -d) + 4) % 4
-        return remote(XS.at[j, m], XR.at[j, m], x_s.at[j, m], x_r.at[j, m], (zl * 16 + y * 4 + to, hd))
+        _, _, turned, _, x1 = which(j)
+        to = (x1 + (way(j) if m != 1 else -way(j)) + 4) % 4
+        dev = zl * 16 + jnp.where(turned, to * 4 + x, y * 4 + to)
+        return remote(XS.at[j, m], XR.at[j, m], x_s.at[j, m], x_r.at[j, m], (dev, hd))
 
     def z_copy(h):
         return remote(ZS.at[h], ZR.at[h], z_s.at[h], z_r.at[h], ((t + 16) % NT, hd))
 
     def step1(j):
-        g, h, d = which(j)
-        YS[j, 0] = part(g, (y + 2) % 4, h).astype(BF)
+        y1 = which(j)[3]
+        YS[j, 0] = part(j, (y1 + 2) % 4).astype(BF)
         y_copy(j, 0).start()
-        YS[j, 1] = part(g, (y - d + 4) % 4, h).astype(BF)
+        YS[j, 1] = part(j, (y1 - way(j) + 4) % 4).astype(BF)
         y_copy(j, 1).start()
 
     def step2(j):
-        g, h, d = which(j)
-        own = part(g, (y + d + 4) % 4, h)
+        own = part(j, (which(j)[3] + way(j) + 4) % 4)
         y_copy(j, 0).wait_recv()
         YS[j, 2] = (own + YR[j, 0].astype(F32)).astype(BF)
         y_copy(j, 2).start()
@@ -304,17 +383,17 @@
         return pl.ds(pl.multiple_of(xx * XB, XB), XB)
 
     def step3(j):
-        g, h, d = which(j)
-        own = part(g, y, h)
+        _, _, _, y1, x1 = which(j)
+        own = part(j, y1)
         y_copy(j, 1).wait_recv()
         y_copy(j, 2).wait_recv()
         YSUM[...] = own + YR[j, 1].astype(F32) + YR[j, 2].astype(F32)
-        XS[j, 0] = YSUM[x_rows((x + 2) % 4)].astype(BF)
+        XS[j, 0] = YSUM[x_rows((x1 + 2) % 4)].astype(BF)
         x_copy(j, 0).start()
-        XS[j, 1] = YSUM[x_rows((x - d + 4) % 4)].astype(BF)
+        XS[j, 1] = YSUM[x_rows((x1 - way(j) + 4) % 4)].astype(BF)
         x_copy(j, 1).start()
-        XK[j, 0] = YSUM[x_rows((x + d + 4) % 4)]
-        XK[j, 1] = YSUM[x_rows(x)]
+        XK[j, 0] = YSUM[x_rows((x1 + way(j) + 4) % 4)]
+        XK[j, 1] = YSUM[x_rows(x1)]
 
     def step4(j):
         x_copy(j, 0).wait_recv()
@@ -322,7 +401,7 @@
         x_copy(j, 2).start()
 
     def step5(j):
-        g, h, _ = which(j)
+        g, h, _, _, _ = which(j)
         x_copy(j, 1).wait_recv()
         x_copy(j, 2).wait_recv()
         ZF[g, h] = XK[j, 1] + XR[j, 1].astype(F32) + XR[j, 2].astype(F32)
@@ -334,31 +413,32 @@
 
     def step6(h):
         z_copy(h).wait_recv()
-        WO[h] = ZF[zl, h] + ZR[h].astype(F32)
+        at = pl.ds(pl.multiple_of(h * HD, HD), HD)
+        WO[at] = (ZF[zl, h] + ZR[h].astype(F32)).T
 
     def turn(j, _):
-        @pl.when(j < GC)
-        def _():
-            zg_wait(j)
-            cf_copy(j).start()
+        for at, mine, onward, arrival in kv_relays():
+            when(mine & (j == at), arrival.wait_recv)
+            when(mine & (j == at), onward.start)
+
+        @pl.when((j >= 2) & (j < GC + 2))
+        def _():
+            cf_wait(j - 2)
+            use_rows(far_mate, j - 2)
 
         @pl.when(j < H)
         def _():
-            for n in range(2):
-                remote(
-                    KV.at[n, j, pl.ds(0, L)], KV.at[n, j, pl.ds(0, L)],
-                    kv_s.at[n, j], kv_r.at[n, j], ((t + 1) % NT, hd),
-                ).wait_recv()
+            @pl.when(t > 0)
+            def _():
+                for n in range(2):
+                    place = KV.at[n, j, pl.ds(0, L)]
+                    remote(place, place, kv_s.at[n, j], kv_r.at[n, j], ((t + 1) % NT, hd)).wait_recv()
+
             forward(j)
 
-        @pl.when(j == H)
-        def _():
-            use_block(far, False)
-            for r in range(GC):
-                cf_wait(r)
-            use_block(far_mate, False)
-            for h in range(H):
-                DO[h] = GA[:, h * HD : (h + 1) * HD].astype(BF)
+        @pl.when((j >= H) & (j < 2 * H))
+        def _():
+            backward(j - H)
 
         @pl.when(j < 2 * H)
         def _():
@@ -368,9 +448,11 @@
         def _():
             step2(j - 1)
 
-        @pl.when((j >= H) & (j < 2 * H))
-        def _():
-            backward(j - H)
+        @pl.when((j >= 1) & (j < GC + 1))
+        def _():
+            zg_wait(j - 1)
+            cf_copy(j - 1).start()
+            use_rows(far, j - 1)
 
         @pl.when((j >= 2) & (j < 2 * H + 2))
         def _():
@@ -380,9 +462,15 @@
         def _():
             step4(j - 3)
 
-        @pl.when((j >= H + 2) & (j < 2 * H + 2))
-        def _():
-            finish_kv(j - H - 2)
+        @pl.when(row_relay_back & (j >= 2 * H) & (j < 2 * H + 2))
+        def _():
+            h = j - 2 * H + 3
+            remote(RLD.at[h - 3], RLD.at[h - 3], rd_s.at[h - 3], rd_r.at[h - 3], (t, hd)).wait_recv()
+            d_onward(h).start()
+
+        @pl.when((j >= H + 3) & (j < 2 * H + 3))
+        def _():
+            finish_kv(j - H - 3)
 
         @pl.when((j >= 4) & (j < 2 * H + 4))
         def _():
@@ -398,6 +486,7 @@
     put_w = pltpu.make_async_copy(WO, wo_ref, w_sem.at[4])
     put_w.start()
 
+    when(zl == 0, over.wait_send)
     co_copy.wait_send()
     for r in range(GC):
         zg_copy(r).wait_send()
@@ -409,13 +498,13 @@
             remote(piece(RB, i), piece(SB, i), sc_s.at[i], sc_r, (i, hd)).wait_send()
             return 0
 
-        lax.fori_loop(1, NT, sent, 0)
+        lax.fori_loop(1, NP, sent, 0)
 
     def ag_sent(i, _):
         ag_copy(i).wait_send()
         return 0
 
-    lax.fori_loop(1, NT, ag_sent, 0)
+    lax.fori_loop(1, NP, ag_sent, 0)
 
     def rs_sent(j, _):
         for m in range(3):
@@ -425,13 +514,33 @@
 
     lax.fori_loop(0, 2 * H, rs_sent, 0)
     for h in range(H):
-        kv_copy(0, h).wait_send()
-        kv_copy(1, h).wait_send()
+        for n in range(2):
+            for condition, copy in kv_copies(n, h):
+                when(condition, copy.wait_send)
         z_copy(h).wait_send()
-        d_copy(h).wait_send()
+        when(t > 0, d_direct(h).wait_send)
         for n in range(3):
             out_copy(n, h).wait()
+    for _, mine, onward, _ in kv_relays():
+        when(mine, onward.wait_send)
+    for h in (3, 4):
+        when(row_relay_back, d_onward(h).wait_send)
     put_w.wait()
+
+
+def hand_over(a, b, c, d, a_out, b_out, c_out, d_out, a_mid, b_mid, c_mid, d_mid, sem):
+    arrays = ((a, a_mid, a_out), (b, b_mid, b_out), (c, c_mid, c_out), (d, d_mid, d_out))
+    copies = [
+        (pltpu.make_async_copy(src, mid, sem.at[0, i]), pltpu.make_async_copy(mid, dst, sem.at[1, i]))
+        for i, (src, mid, dst) in enumerate(arrays)
+    ]
+    for load, _ in copies:
+        load.start()
+    for load, store in copies:
+        load.wait()
+        store.start()
+    for _, store in copies:
+        store.wait()
 
 
 def per_device(query, key, value, out_weight, grad_out, sink_frame, window):
@@ -441,7 +550,7 @@
     sds = jax.ShapeDtypeStruct
     grad_query, grad_key, grad_value, weight = pl.pallas_call(
         kernel,
-        out_shape=[sds((L, H * HD), BF)] * 3 + [sds((H, XB, HD), F32)],
+        out_shape=[sds((L, H * HD), BF)] * 3 + [sds((H * HD, XB), F32)],
         in_specs=[any_spec] * 5 + [smem] * 2,
         out_specs=[any_spec] * 4,
         scratch_shapes=[
@@ -449,11 +558,12 @@
             pltpu.VMEM((2, H, 2 * L, HD), BF),
             pltpu.VMEM((2, H, T, HD), BF),
             pltpu.VMEM((2, H, T, HD), BF),
+            pltpu.VMEM((2, 2, L, HD), BF),
+            pltpu.VMEM((2, 2, L, HD), BF),
             pltpu.VMEM((4, L, CW), BF),
-            pltpu.VMEM((8, YB, L), BF),
+            pltpu.VMEM((8, 4, XB, L), BF),
             pltpu.VMEM((4, H * HD, CW), BF),
             pltpu.VMEM((L, H * HD), F32),
-            pltpu.VMEM((H, L, HD), BF),
             pltpu.VMEM((2 * H, 4 * T, T), F32),
             pltpu.VMEM((H, HD, L), BF),
             pltpu.VMEM((2 * H, 3, YB, HD), BF),
@@ -465,18 +575,18 @@
             pltpu.VMEM((2, H, XB, HD), F32),
             pltpu.VMEM((H, XB, HD), BF),
             pltpu.VMEM((H, XB, HD), BF),
-            pltpu.VMEM((H, XB, HD), F32),
+            pltpu.VMEM((H * HD, XB), F32),
             pltpu.VMEM((H, 2, L, HD), BF),
             pltpu.VMEM((H, 2, L, HD), BF),
             pltpu.VMEM((H, L, HD), BF),
             pltpu.VMEM((2, H, L, HD), BF),
             dma((3 * H,)), dma((5,)),
-            dma((2, H)), dma((2, H)),
+            dma((2, H)), dma((2, H)), dma((2, 2)), dma((2, 2)), dma((2,)), dma((2,)),
             dma((GC,)), dma((GC,)),
             dma, dma,
             dma((GC,)), dma((GC,)),
             dma((NT,)), dma,
-            dma((NT,)), dma((NT,)),
+            dma((NP,)), dma((NP,)),
             dma((2 * H, 3)), dma((2 * H, 3)),
             dma((2 * H, 3)), dma((2 * H, 3)),
             dma((H,)), dma((H,)),
@@ -488,8 +598,18 @@
         ),
         name="layer_backward",
     )(query, key, value, out_weight, grad_out, sink_frame, window)
-    grad_weight = jnp.swapaxes(weight, 1, 2).reshape(H * HD, XB)
-    return (grad_query, grad_key, grad_value, grad_weight)
+    outs = [sds((L, H * HD), BF)] * 3 + [sds((H * HD, XB), F32)]
+    return tuple(
+        pl.pallas_call(
+            hand_over,
+            out_shape=outs,
+            in_specs=[any_spec] * 4,
+            out_specs=[any_spec] * 4,
+            scratch_shapes=[pltpu.VMEM(o.shape, o.dtype) for o in outs] + [dma((2, 4))],
+            compiler_params=pltpu.CompilerParams(vmem_limit_bytes=60 * 1024 * 1024),
+            name="hand_over",
+        )(grad_query, grad_key, grad_value, weight)
+    )
 
 
 def solution(mesh):

time: 194 us -> 139 us (0.72)
  the two profiles are of different devices: /device:TPU:96 before, /device:TPU:6 now
where the time goes in v2:
time: 139 us; the launch traced here: 138 us
  Pallas kernels  136 us (98%)
  local copies, waits for them, and re-layouts  2.05 us (1%)
    pallas_call x1, Pallas kernels, per_device(): pl.pallas_call(kernel, out_shape=[sds((L, H * HD), BF)] * 3 + [sds((H * H...  133 us

profile of v2, /device:TPU:6, one launch (start us, length us, event | category | flops | bytes accessed | tf_op | source)
XLA Modules:
  0.0 138.4 jit_solution(6415885498546017347)
XLA Ops:
  0.6 133.1 %layer_backward.1 = (bf16[512,640]{1,0:T(8,128)(2,1)}, bf16[512,640]{1,0:T(8,128)(2,1)}, bf16[512,640]{1,0:T(8,128)(2,1)}, f32[640,160]{1,0:T(8,128)}) custom-call(bf16[512,640]{1,0:T(8,128)(2,1)} %q_ref.1, bf16[512,640]{1,0:T(8,128)(2,1)} %k_ref.1, bf16[512,640]{1,0:T(8,128)(2,1)} %v_ref.1, bf16[640,5120]{1,0:T(8,128)(2,1)} %w_ref.1, ...), custom_call_target="tpu_custom_call" | custom-call | tf_op jit(solution)/shard_map/layer_backward/pallas_call | solution.py:551
  133.7 2.6 %hand_over.1 = (bf16[512,640]{1,0:T(8,128)(2,1)}, bf16[512,640]{1,0:T(8,128)(2,1)}, bf16[512,640]{1,0:T(8,128)(2,1)}, f32[640,160]{1,0:T(8,128)}) custom-call(bf16[512,640]{1,0:T(8,128)(2,1)} %get-tuple-element.8.a, bf16[512,640]{1,0:T(8,128)(2,1)} %get-tuple-element.9.b, bf16[512,640]{1,0:T(8,128)(2,1)} %get-tuple-element.10.c, f32[640,160]{1,0:T(8,128)} %get-tuple-element.11.d), custom_call_target="tpu_custom_call" | custom-call | tf_op jit(solution)/shard_map/hand_over/pallas_call | solution.py:603
  136.4 2.0 %copy.11 = f32[640,160]{0,1:T(8,128)} copy(f32[640,160]{1,0:T(8,128)} %get-tuple-element.15) | data formatting | bytes 819200 | tf_op jit(solution)/shard_map/hand_over/pallas_call | solution.py:603

commit v3 on v2

--- a/solution.py
+++ b/solution.py
@@ -26,7 +26,7 @@
 EARLY_ZG = 0
 Z_RELAY = {1: 17, 2: 20, 3: 28, 4: 19}
 X_FIRST = (1, 3)
-EARLY_PLUS = 3
+LAG2, LAG3, LAG4, LAG5, LAG6 = 1, 2, 3, 4, 5
 
 
 def mm(a, b):
@@ -342,7 +342,7 @@
         return (zh + j // H) % 2, h, turned, jnp.where(turned, x, y), jnp.where(turned, y, x)
 
     def way(j):
-        return jnp.where((j < H) & (j != EARLY_PLUS), -1, 1)
+        return jnp.where((j < H) & (j != 3), -1, 1)
 
     def part(j, at):
         g, h, turned, _, _ = which(j)
@@ -436,17 +436,13 @@
 
             forward(j)
 
-        @pl.when((j >= H) & (j < 2 * H))
-        def _():
-            backward(j - H)
-
         @pl.when(j < 2 * H)
         def _():
             step1(j)
 
-        @pl.when((j >= 1) & (j < 2 * H + 1))
-        def _():
-            step2(j - 1)
+        @pl.when((j >= LAG2) & (j < 2 * H + LAG2))
+        def _():
+            step2(j - LAG2)
 
         @pl.when((j >= 1) & (j < GC + 1))
         def _():
@@ -454,13 +450,17 @@
             cf_copy(j - 1).start()
             use_rows(far, j - 1)
 
-        @pl.when((j >= 2) & (j < 2 * H + 2))
-        def _():
-            step3(j - 2)
-
-        @pl.when((j >= 3) & (j < 2 * H + 3))
-        def _():
-            step4(j - 3)
+        @pl.when((j >= H) & (j < 2 * H))
+        def _():
+            backward(j - H)
+
+        @pl.when((j >= LAG3) & (j < 2 * H + LAG3))
+        def _():
+            step3(j - LAG3)
+
+        @pl.when((j >= LAG4) & (j < 2 * H + LAG4))
+        def _():
+            step4(j - LAG4)
 
         @pl.when(row_relay_back & (j >= 2 * H) & (j < 2 * H + 2))
         def _():
@@ -468,21 +468,21 @@
             remote(RLD.at[h - 3], RLD.at[h - 3], rd_s.at[h - 3], rd_r.at[h - 3], (t, hd)).wait_recv()
             d_onward(h).start()
 
-        @pl.when((j >= H + 3) & (j < 2 * H + 3))
-        def _():
-            finish_kv(j - H - 3)
-
-        @pl.when((j >= 4) & (j < 2 * H + 4))
-        def _():
-            step5(j - 4)
-
-        @pl.when(j >= H + 5)
-        def _():
-            step6(j - H - 5)
+        @pl.when((j >= H + 5) & (j < 2 * H + 5))
+        def _():
+            finish_kv(j - H - 5)
+
+        @pl.when((j >= LAG5) & (j < 2 * H + LAG5))
+        def _():
+            step5(j - LAG5)
+
+        @pl.when(j >= H + LAG6)
+        def _():
+            step6(j - H - LAG6)
 
         return 0
 
-    lax.fori_loop(0, 2 * H + 5, turn, 0)
+    lax.fori_loop(0, 2 * H + LAG6, turn, 0)
     put_w = pltpu.make_async_copy(WO, wo_ref, w_sem.at[4])
     put_w.start()
 

time: 139 us -> 135 us (0.971)
  the two profiles are of different devices: /device:TPU:6 before, /device:TPU:96 now
where the time goes in v3:
time: 135 us; the launch traced here: 133 us
  Pallas kernels  130 us (96%)
  local copies, waits for them, and re-layouts  2.05 us (2%)
    pallas_call x1, Pallas kernels, per_device(): pl.pallas_call(kernel, out_shape=[sds((L, H * HD), BF)] * 3 + [sds((H * H...  127 us

profile of v3, /device:TPU:96, one launch (start us, length us, event | category | flops | bytes accessed | tf_op | source)
XLA Modules:
  0.0 132.7 jit_solution(15515114600432342035)
XLA Ops:
  0.6 127.3 %layer_backward.1 = (bf16[512,640]{1,0:T(8,128)(2,1)}, bf16[512,640]{1,0:T(8,128)(2,1)}, bf16[512,640]{1,0:T(8,128)(2,1)}, f32[640,160]{1,0:T(8,128)}) custom-call(bf16[512,640]{1,0:T(8,128)(2,1)} %q_ref.1, bf16[512,640]{1,0:T(8,128)(2,1)} %k_ref.1, bf16[512,640]{1,0:T(8,128)(2,1)} %v_ref.1, bf16[640,5120]{1,0:T(8,128)(2,1)} %w_ref.1, ...), custom_call_target="tpu_custom_call" | custom-call | tf_op jit(solution)/shard_map/layer_backward/pallas_call | solution.py:551
  128.0 2.6 %hand_over.1 = (bf16[512,640]{1,0:T(8,128)(2,1)}, bf16[512,640]{1,0:T(8,128)(2,1)}, bf16[512,640]{1,0:T(8,128)(2,1)}, f32[640,160]{1,0:T(8,128)}) custom-call(bf16[512,640]{1,0:T(8,128)(2,1)} %get-tuple-element.8.a, bf16[512,640]{1,0:T(8,128)(2,1)} %get-tuple-element.9.b, bf16[512,640]{1,0:T(8,128)(2,1)} %get-tuple-element.10.c, f32[640,160]{1,0:T(8,128)} %get-tuple-element.11.d), custom_call_target="tpu_custom_call" | custom-call | tf_op jit(solution)/shard_map/hand_over/pallas_call | solution.py:603
  130.6 2.0 %copy.11 = f32[640,160]{0,1:T(8,128)} copy(f32[640,160]{1,0:T(8,128)} %get-tuple-element.15) | data formatting | bytes 819200 | tf_op jit(solution)/shard_map/hand_over/pallas_call | solution.py:603

commit v4 on v3

--- a/solution.py
+++ b/solution.py
@@ -77,13 +77,29 @@
     barrier = pltpu.get_barrier_semaphore()
 
     def greet(i, _):
-        pl.semaphore_signal(barrier, inc=1, device_id=((t + i) % NT, hd), device_id_type=MESH)
+        to = zl * NP + (t + i) % NP
+        pl.semaphore_signal(barrier, inc=1, device_id=(to, hd), device_id_type=MESH)
         return 0
 
-    lax.fori_loop(1, NT, greet, 0)
+    lax.fori_loop(1, NP, greet, 0)
+    pl.semaphore_signal(barrier, inc=1, device_id=((t + NP) % NT, hd), device_id_type=MESH)
+    crossing = (NP, *Z_RELAY.values())
+    for at in crossing:
+
+        @pl.when(t == NP - 1)
+        def _():
+            pl.semaphore_signal(barrier, inc=1, device_id=(at, hd), device_id_type=MESH)
+
+        @pl.when(t == at)
+        def _():
+            pl.semaphore_signal(barrier, inc=1, device_id=(NP - 1, hd), device_id_type=MESH)
+
     pl.semaphore_signal(barrier, inc=1, device_id=(t, mate), device_id_type=MESH)
     pl.semaphore_signal(barrier, inc=1, device_id=(t, far), device_id_type=MESH)
-    pl.semaphore_wait(barrier, NT + 1)
+    met = jnp.where(t == NP - 1, len(crossing), 0)
+    for at in crossing:
+        met = met + jnp.where(t == at, 1, 0)
+    pl.semaphore_wait(barrier, NP + 2 + met)
 
     row_end = (x == 3) & (y < 3)
     plane_end = t == NT // 2 - 1

time: 135 us -> 134 us (level)
  no operation moved by 1% of the time
where the time goes in v4:
time: 134 us; the launch traced here: 132 us
  Pallas kernels  129 us (96%)
  local copies, waits for them, and re-layouts  2.05 us (2%)
    pallas_call x1, Pallas kernels, per_device(): pl.pallas_call(kernel, out_shape=[sds((L, H * HD), BF)] * 3 + [sds((H * H...  126 us

profile of v4, /device:TPU:96, one launch (start us, length us, event | category | flops | bytes accessed | tf_op | source)
XLA Modules:
  0.0 131.6 jit_solution(11158407744920272635)
XLA Ops:
  0.6 126.3 %layer_backward.1 = (bf16[512,640]{1,0:T(8,128)(2,1)}, bf16[512,640]{1,0:T(8,128)(2,1)}, bf16[512,640]{1,0:T(8,128)(2,1)}, f32[640,160]{1,0:T(8,128)}) custom-call(bf16[512,640]{1,0:T(8,128)(2,1)} %q_ref.1, bf16[512,640]{1,0:T(8,128)(2,1)} %k_ref.1, bf16[512,640]{1,0:T(8,128)(2,1)} %v_ref.1, bf16[640,5120]{1,0:T(8,128)(2,1)} %w_ref.1, ...), custom_call_target="tpu_custom_call" | custom-call | tf_op jit(solution)/shard_map/layer_backward/pallas_call | solution.py:567
  126.9 2.6 %hand_over.1 = (bf16[512,640]{1,0:T(8,128)(2,1)}, bf16[512,640]{1,0:T(8,128)(2,1)}, bf16[512,640]{1,0:T(8,128)(2,1)}, f32[640,160]{1,0:T(8,128)}) custom-call(bf16[512,640]{1,0:T(8,128)(2,1)} %get-tuple-element.8.a, bf16[512,640]{1,0:T(8,128)(2,1)} %get-tuple-element.9.b, bf16[512,640]{1,0:T(8,128)(2,1)} %get-tuple-element.10.c, f32[640,160]{1,0:T(8,128)} %get-tuple-element.11.d), custom_call_target="tpu_custom_call" | custom-call | tf_op jit(solution)/shard_map/hand_over/pallas_call | solution.py:619
  129.6 2.0 %copy.11 = f32[640,160]{0,1:T(8,128)} copy(f32[640,160]{1,0:T(8,128)} %get-tuple-element.15) | data formatting | bytes 819200 | tf_op jit(solution)/shard_map/hand_over/pallas_call | solution.py:619
